TPU v7x, 256 devices: a whole 4x4x8 slice. The times are simulated.
256 devices in a mesh: pipe: 8 (over z), tp: 32 (over y, x, core).
Axes of the slice: x: 4, y: 4, z: 8, core: 2. Of those that a mesh axis runs over, the one named last changes fastest.
Arguments:
- x_prev: bfloat16 [8, 128, 12288], P('pipe', None, 'tp'), may hold values from -6 to 6
- x_saved: bfloat16 [8, 128, 12288], P('pipe', None, 'tp'), may hold values from -6 to 6
- g_next: bfloat16 [8, 128, 12288], P('pipe', None, 'tp'), may hold values from -6 to 6
- w_qkv: bfloat16 [8, 12288, 32, 384], P('pipe', None, 'tp'), may hold values from -0.0546875 to 0.0546875
- w_out: bfloat16 [8, 4096, 12288], P('pipe', 'tp'), may hold values from -0.09375 to 0.09375
- gain: float32 [8, 12288], P('pipe'), may hold values from 0.5 to 1.5
- doc_ids: int32 [8, 2, 128], P('pipe'), may hold values from 0 to 3, never falling along the last dimension, each value on 1 to 64 neighbouring positions
Outputs:
- y_out: bfloat16 [8, 128, 12288], P('pipe', None, 'tp')
- section_input_gradient: bfloat16 [8, 128, 12288], P('pipe', None, 'tp')
Inputs may be any that keep to these rules, and one draw needn't show every extreme that they name: `doc_ids`: document ids never fall along a micro-batch; each document holds 1 to 64 tokens and one holds exactly that many.
All inputs are finite; a program needn't handle non-finite values.
Results may differ from a plain program's by a relative error of at most 0.019.
Values may be sent and summed in bfloat16 or wider, within the bound.
A program may use at most 128 MiB of HBM per device.

v0:
```python
import math

import jax
import jax.numpy as jnp
from jax import lax
from jax.sharding import PartitionSpec as P

D = 12288
HEAD_DIM = 128


EPS = 1e-05


def shifted(value, axis, by):
    size = lax.axis_size(axis)
    return lax.ppermute(value, axis, [(i, (i + by) % size) for i in range(size)])


def layer_stats(inputs):
    values = inputs.astype(jnp.float32)
    center = jnp.mean(values, -1, keepdims=True)
    square = jnp.mean(values * values, -1, keepdims=True)
    inv_std = lax.rsqrt(square - center * center + EPS)
    x_hat = (values - center) * inv_std
    return (x_hat, inv_std)


def build_mask(doc_row):
    positions = jnp.arange(doc_row.shape[0], dtype=jnp.int32)
    return (positions[None, :] <= positions[:, None]) & (doc_row[:, None] == doc_row[None, :])


def attend(queries, key_rows, value_rows, visible):
    scaling = 1.0 / math.sqrt(HEAD_DIM)
    scores = (
        jnp.einsum("qhe,khe->hqk", queries, key_rows, preferred_element_type=jnp.float32) * scaling
    )
    scores = jnp.where(visible[None], scores, -1e30)
    highest = jnp.max(scores, -1, keepdims=True)
    exponent = jnp.exp(scores - highest)
    attn_probs = exponent / jnp.sum(exponent, -1, keepdims=True)
    probs_low = attn_probs.astype(jnp.bfloat16)
    mixed = jnp.einsum("hqk,khe->qhe", probs_low, value_rows, preferred_element_type=jnp.float32)
    return (mixed.astype(jnp.bfloat16), attn_probs, probs_low)


def norm_backward(
    hidden_gradient, gain_forward_copy, normed_input_backward, reciprocal_deviation_backward
):
    normed_input_gradient = hidden_gradient * gain_forward_copy
    gradient_average = jnp.mean(normed_input_gradient, -1, keepdims=True)
    gradient_projected_dot = jnp.mean(
        normed_input_gradient * normed_input_backward, -1, keepdims=True
    )
    return reciprocal_deviation_backward * (
        normed_input_gradient - gradient_average - normed_input_backward * gradient_projected_dot
    )


def shards(x_prev, x_saved, g_next, w_qkv, w_out, gain, doc_ids):
    x_in = shifted(x_prev, "pipe", 1)[0]
    incoming_gradient = shifted(g_next, "pipe", -1)[0]
    x_back = x_saved[0]
    local_heads = w_qkv.shape[2]
    weights = w_qkv[0].reshape(D, local_heads * 3 * HEAD_DIM)
    w_proj = w_out[0]
    gain_forward_copy = gain[0]
    doc_rows = doc_ids[0]
    row_count = x_in.shape[0]
    feat_width = x_in.shape[1]
    head_cols = local_heads * HEAD_DIM
    contract_last = (((1,), (1,)), ((), ()))
    full_in, full_back = (
        lax.all_gather(x_in, "tp", axis=1, tiled=True),
        lax.all_gather(x_back, "tp", axis=1, tiled=True),
    )
    x_hat_f, inv_std_f = layer_stats(full_in)
    hidden_f = (x_hat_f * gain_forward_copy).astype(jnp.bfloat16)
    qkv_f = jnp.dot(hidden_f, weights, preferred_element_type=jnp.float32).astype(jnp.bfloat16)
    qkv_f = qkv_f.reshape(row_count, local_heads, 3, HEAD_DIM)
    mixed_f = attend(qkv_f[:, :, 0], qkv_f[:, :, 1], qkv_f[:, :, 2], build_mask(doc_rows[0]))[0]
    mixed_f = mixed_f.reshape(row_count, head_cols)
    projected = jnp.dot(mixed_f, w_proj, preferred_element_type=jnp.float32)
    added = lax.psum_scatter(
        projected.astype(jnp.bfloat16), "tp", scatter_dimension=1, tiled=True
    ).astype(jnp.float32)
    y_out = (x_in.astype(jnp.float32) + added).astype(jnp.bfloat16)
    normed_input_backward, reciprocal_deviation_backward = layer_stats(full_back)
    hidden_b = (normed_input_backward * gain_forward_copy).astype(jnp.bfloat16)
    qkv_b = jnp.dot(hidden_b, weights, preferred_element_type=jnp.float32).astype(jnp.bfloat16)
    qkv_b = qkv_b.reshape(row_count, local_heads, 3, HEAD_DIM)
    queries, key_rows, value_rows = (qkv_b[:, :, 0], qkv_b[:, :, 1], qkv_b[:, :, 2])
    mixed_b, attn_probs, probs_low = attend(queries, key_rows, value_rows, build_mask(doc_rows[1]))
    d_out = lax.dot_general(
        lax.all_gather(incoming_gradient, "tp", axis=1, tiled=True),
        w_proj,
        contract_last,
        preferred_element_type=jnp.float32,
    ).astype(jnp.bfloat16)
    d_three = d_out.reshape(row_count, local_heads, HEAD_DIM)
    d_values = jnp.einsum(
        "hqk,qhe->khe", probs_low, d_three, preferred_element_type=jnp.float32
    ).astype(jnp.bfloat16)
    d_probs = jnp.einsum("qhe,khe->hqk", d_three, value_rows, preferred_element_type=jnp.float32)
    d_scores = (
        attn_probs
        * (d_probs - jnp.sum(d_probs * attn_probs, -1, keepdims=True))
        / math.sqrt(HEAD_DIM)
    ).astype(jnp.bfloat16)
    d_query = jnp.einsum(
        "hqk,khe->qhe", d_scores, key_rows, preferred_element_type=jnp.float32
    ).astype(jnp.bfloat16)
    d_keys = jnp.einsum(
        "hqk,qhe->khe", d_scores, queries, preferred_element_type=jnp.float32
    ).astype(jnp.bfloat16)
    d_qkv = jnp.stack([d_query, d_keys, d_values], 2).reshape(row_count, 3 * head_cols)
    d_partial = lax.dot_general(d_qkv, weights, contract_last, preferred_element_type=jnp.float32)
    hidden_gradient = lax.psum(d_partial.astype(jnp.bfloat16), "tp").astype(jnp.float32)
    all_terms = norm_backward(
        hidden_gradient, gain_forward_copy, normed_input_backward, reciprocal_deviation_backward
    )
    own_terms = lax.dynamic_slice_in_dim(
        all_terms, lax.axis_index("tp") * feat_width, feat_width, 1
    )
    section_input_gradient = (incoming_gradient.astype(jnp.float32) + own_terms).astype(
        jnp.bfloat16
    )
    return (y_out[None], section_input_gradient[None])


def solution(mesh):
    in_specs = (
        P("pipe", None, "tp"),
        P("pipe", None, "tp"),
        P("pipe", None, "tp"),
        P("pipe", None, "tp", None),
        P("pipe", "tp", None),
        P("pipe", None),
        P("pipe", None, None),
    )
    out_specs = (P("pipe", None, "tp"), P("pipe", None, "tp"))
    return jax.shard_map(shards, mesh=mesh, in_specs=in_specs, out_specs=out_specs, check_vma=False)
```

profile of v0, /device:TPU:2, one launch (start us, length us, event | category | flops | bytes accessed | tf_op | source)
XLA Modules:
  0.0 396.4 jit_solution(13603304955659099953)
XLA Ops:
  7.2 0.7 all-gather.9.cloned.1.call-update
  8.0 5.9 %collective-permute-start.1 = (bf16[1,128,384]{2,1,0:T(8,128)(2,1)}, bf16[1,128,384]{2,1,0:T(8,128)(2,1)S(1)}, u32[]{:S(2)}, u32[]{:S(2)}) collective-permute-start(bf16[1,128,384]{2,1,0:T(8,128)(2,1)} %param.9), channel_id=1, source_target_pairs={{0,224},{32,0},{64,32},{96,64},{128,96},{160,128},{192,160},{224,1... | collective-permute-start | bytes 294920 | tf_op jit(solution)/shard_map/ppermute | solution.py:17
  13.9 2.5 collective-permute-done.1
  16.4 0.6 copy-done.3
  17.2 6.3 %collective-permute-done = bf16[1,128,384]{2,1,0:T(8,128)(2,1)S(1)} collective-permute-done((bf16[1,128,384]{2,1,0:T(8,128)(2,1)}, bf16[1,128,384]{2,1,0:T(8,128)(2,1)S(1)}, u32[]{:S(2)}, u32[]{:S(2)}) %collective-permute-start) | collective-permute-done | bytes 98336 | tf_op jit(solution)/shard_map/ppermute | solution.py:17
  23.5 0.6 copy-done.5
  24.3 0.8 slice_bitcast_fusion.15
  25.0 40.0 %all-gather.9.cloned.1.call-done = bf16[1,128,12288]{2,1,0:T(8,128)(2,1)} async-done(((bf16[1,128,384]{2,1,0:T(8,128)(2,1)}), bf16[1,128,12288]{2,1,0:T(8,128)(2,1)}) %all-gather.9.cloned.1.call-update) | async-done | bytes 3145744 | tf_op jit(solution)/shard_map/all_gather | solution.py:76
  65.1 2.5 convert_reduce_fusion
  67.6 2.6 fusion.13
  70.2 5.5 %fusion.30 = bf16[128,384]{1,0:T(8,128)(2,1)S(1)} fusion(bf16[1,12288,1,384]{3,1,2,0:T(8,128)(2,1)} %param.10, f32[12288]{0:T(1024)S(1)} %bitcast.154, bf16[1,128,12288]{2,1,0:T(8,128)(2,1)S(1)} %copy-done.1, f32[128]{0:T(128)S(1)} %get-tuple-element.9, f32[128]{0:T(128)S(1)} %get-tuple-element.8), kind=kOutput, calls=%fused_computation.34 | convolution fusion | flops 1215873024 | bytes 12731392 | tf_op jit(solution)/shard_map/dot_general | solution.py:91
  75.9 0.2 fusion.65
  76.2 43.4 %all-gather.11.cloned.1.call-done = bf16[1,128,12288]{2,1,0:T(8,128)(2,1)} async-done(((bf16[1,128,384]{2,1,0:T(8,128)(2,1)}), bf16[1,128,12288]{2,1,0:T(8,128)(2,1)}) %all-gather.11.cloned.1.call-update) | async-done | bytes 3145744 | tf_op jit(solution)/shard_map/all_gather | solution.py:96
  119.5 2.9 fusion.35
  122.4 0.2 multiply_reduce_fusion.1
  122.8 0.1 fusion.42
  122.9 0.2 fusion.43
  123.2 8.5 %convolution_convert_fusion = bf16[128,12288]{1,0:T(8,128)(2,1)} fusion(bf16[128,384]{0,1:T(8,128)(2,1)S(1)} %bitcast.146, bf16[1,12288,1,384]{3,1,2,0:T(8,128)(2,1)} %param.10), kind=kOutput, calls=%fused_computation | convolution fusion | flops 1209532416 | bytes 12681216 | tf_op jit(solution)/shard_map/dot_general | solution.py:118
  131.7 0.2 reduce-scatter.4.cloned.1.call-start
  132.0 42.1 %all-gather.7.cloned.1.call-done = bf16[1,128,12288]{2,1,0:T(8,128)(2,1)} async-done(((bf16[1,128,384]{2,1,0:T(8,128)(2,1)}), bf16[1,128,12288]{2,1,0:T(8,128)(2,1)}) %all-gather.7.cloned.1.call-update) | async-done | bytes 3145744 | tf_op jit(solution)/shard_map/all_gather | solution.py:75
  174.1 2.5 convert_reduce_fusion.1
  176.6 2.6 fusion.9
  179.2 5.5 %fusion.25 = bf16[128,384]{1,0:T(8,128)(2,1)S(1)} fusion(bf16[1,12288,1,384]{3,1,2,0:T(8,128)(2,1)} %param.10, bf16[1,128,12288]{2,1,0:T(8,128)(2,1)S(1)} %copy-done.2, f32[12288]{0:T(1024)S(1)} %bitcast.155, f32[128]{0:T(128)S(1)} %get-tuple-element.11, f32[128]{0:T(128)S(1)} %get-tuple-element.10), kind=kOutput, calls=%fused_computation.33 | convolution fusion | flops 1215873024 | bytes 12731392 | tf_op jit(solution)/shard_map/dot_general | solution.py:80
  184.9 0.2 fusion.64
  185.1 2.8 convolution_convert_fusion.1
  188.0 4.7 %copy.25 = bf16[128,12288]{0,1:T(8,128)(2,1)} copy(bf16[128,12288]{1,0:T(8,128)(2,1)} %convolution_convert_fusion.1) | data formatting | bytes 6291456
  192.7 103.7 %all-reduce.2.cloned.1.call-done = bf16[128,12288]{1,0:T(8,128)(2,1)} async-done(((bf16[128,12288]{1,0:T(8,128)(2,1)}), bf16[128,12288]{1,0:T(8,128)(2,1)}) %all-reduce.2.cloned.1.call-update) | async-done | bytes 3145744 | tf_op jit(solution)/shard_map/psum | solution.py:119
  296.4 4.6 %fusion.24 = (f32[128]{0:T(128)S(1)}, f32[128]{0:T(128)S(1)}, f32[128,12288]{1,0:T(8,128)S(1)}, f32[128,12288]{1,0:T(8,128)S(1)}) fusion(f32[12288]{0:T(1024)S(1)} %bitcast.156, bf16[128,12288]{1,0:T(8,128)(2,1)} %all-reduce.2.cloned.1.call-done, f32[128]{0:T(128)S(1)} %get-tuple-element.8, f32[128]{0:T(128)S(1)} %get-tuple-element.9, ...), kind=kLoop, calls=%fused_computation.32 | loop fusion | flops 12582656 | bytes 18925568 | tf_op jit(solution)/shard_map/reduce_sum | solution.py:52
  301.0 0.8 fusion.50
  301.8 86.5 %reduce-scatter.4.cloned.1.call-done = bf16[384,128]{1,0:T(8,128)(2,1)} async-done(((bf16[12288,128]{1,0:T(8,128)(2,1)}), bf16[384,128]{1,0:T(8,128)(2,1)}) %reduce-scatter.4.cloned.1.call-update) | async-done | bytes 98320
  388.2 1.0 copy.26
  389.2 0.7 fusion.49
  (33 shorter events, 0.9 us)
Async XLA Ops:
  7.2 112.4 %copy-start = (bf16[1,128,12288]{2,1,0:T(8,128)(2,1)S(1)}, bf16[1,128,12288]{2,1,0:T(8,128)(2,1)}, u32[]{:S(2)}) copy-start(bf16[1,128,12288]{2,1,0:T(8,128)(2,1)} %param.11) | copy-start | bytes 9437188
  7.2 63.0 %copy-start.7 = (f32[1,12288]{1,0:T(1,128)S(1)}, f32[1,12288]{1,0:T(1,128)}, u32[]{:S(2)}) copy-start(f32[1,12288]{1,0:T(1,128)} %param.12) | copy-start | bytes 147460
  7.2 57.9 %all-gather.9.cloned.1.call-start = ((), (), s32[]{:S(2)}) async-start(), calls=%async_computation.3 | async-start | bytes 3244032 | tf_op jit(solution)/shard_map/all_gather | solution.py:76
  7.9 111.6 %all-gather.11.cloned.1.call-start = ((), (), s32[]{:S(2)}) async-start(), calls=%async_computation.4 | async-start | bytes 3244032 | tf_op jit(solution)/shard_map/all_gather | solution.py:96
  8.0 8.5 %collective-permute-start.1 = (bf16[1,128,384]{2,1,0:T(8,128)(2,1)}, bf16[1,128,384]{2,1,0:T(8,128)(2,1)S(1)}, u32[]{:S(2)}, u32[]{:S(2)}) collective-permute-start(bf16[1,128,384]{2,1,0:T(8,128)(2,1)} %param.9), channel_id=1, source_target_pairs={{0,224},{32,0},{64,32},{96,64},{128,96},{160,128},{192,160},{224,1... | collective-permute-start | bytes 294920 | tf_op jit(solution)/shard_map/ppermute | solution.py:17
  16.4 0.6 copy-start.3
  17.1 156.9 %all-gather.7.cloned.1.call-start = ((), (), s32[]{:S(2)}) async-start(), calls=%async_computation.2 | async-start | bytes 3244032 | tf_op jit(solution)/shard_map/all_gather | solution.py:75
  17.1 6.4 %collective-permute-start = (bf16[1,128,384]{2,1,0:T(8,128)(2,1)}, bf16[1,128,384]{2,1,0:T(8,128)(2,1)S(1)}, u32[]{:S(2)}, u32[]{:S(2)}) collective-permute-start(bf16[1,128,384]{2,1,0:T(8,128)(2,1)} %param.7), channel_id=1, source_target_pairs={{0,32},{32,64},{64,96},{96,128},{128,160},{160,192},{192,224},{224... | collective-permute-start | bytes 294920 | tf_op jit(solution)/shard_map/ppermute | solution.py:17
  23.5 0.6 copy-start.5
  24.2 272.1 %all-reduce.2.cloned.1.call-start = ((), (), s32[]{:S(2)}) async-start(), calls=%async_computation.1 | async-start | bytes 6291456 | tf_op jit(solution)/shard_map/psum | solution.py:119
  65.1 5.1 %copy-start.1 = (bf16[1,128,12288]{2,1,0:T(8,128)(2,1)S(1)}, bf16[1,128,12288]{2,1,0:T(8,128)(2,1)}, u32[]{:S(2)}) copy-start(bf16[1,128,12288]{2,1,0:T(8,128)(2,1)} %all-gather.9.cloned.1.call-done) | copy-start | bytes 9437188
  131.7 256.5 %reduce-scatter.4.cloned.1.call-start = ((), (), s32[]{:S(2)}) async-start(), calls=%async_computation.5 | async-start | bytes 3244032
  174.0 5.1 %copy-start.2 = (bf16[1,128,12288]{2,1,0:T(8,128)(2,1)S(1)}, bf16[1,128,12288]{2,1,0:T(8,128)(2,1)}, u32[]{:S(2)}) copy-start(bf16[1,128,12288]{2,1,0:T(8,128)(2,1)} %all-gather.7.cloned.1.call-done) | copy-start | bytes 9437188
  192.7 108.3 %copy-start.4 = (bf16[1,128,384]{2,1,0:T(8,128)(2,1)S(1)}, bf16[1,128,384]{2,1,0:T(8,128)(2,1)}, u32[]{:S(2)}) copy-start(bf16[1,128,384]{2,1,0:T(8,128)(2,1)} %copy-done.3) | copy-start | bytes 294916
  192.7 196.6 %copy-start.6 = (bf16[1,128,384]{2,1,0:T(8,128)(2,1)S(1)}, bf16[1,128,384]{2,1,0:T(8,128)(2,1)}, u32[]{:S(2)}) copy-start(bf16[1,128,384]{2,1,0:T(8,128)(2,1)} %copy-done.5) | copy-start | bytes 294916
Sparse Core Ops, SparseCore 0:
  10.5 54.5 all-gather.8
  68.1 51.4 all-gather.10
  122.6 51.4 all-gather.6
  177.2 119.0 all-reduce.1
  300.1 88.0 reduce-scatter.3
where the time goes:
time: 397 us; the launch traced here: 396 us
  waiting for transfers between devices  325 us (82%)
  matrix products  26.5 us (7%)
  other arithmetic  16.4 us (4%)
  between operations  14 us (4%)
  local copies, waits for them, and re-layouts  7.97 us (2%)
  starting transfers between devices  6.4 us (2%)
    psum x1, waiting for transfers between devices, shards(): lax.psum(d_partial.astype(jnp.bfloat16), 'tp').astype(jnp.float32)  104 us
    unnamed x6, waiting for transfers between devices  87.2 us
    all_gather x1, waiting for transfers between devices, shards(): lax.all_gather(incoming_gradient, 'tp', axis=1, tiled=True)  43.4 us
    all_gather x1, waiting for transfers between devices, shards(): lax.all_gather(x_in, 'tp', axis=1, tiled=True)  42.1 us
    all_gather x1, waiting for transfers between devices, shards(): lax.all_gather(x_back, 'tp', axis=1, tiled=True)  40 us
    ppermute x2, waiting for transfers between devices, shifted(): lax.ppermute(value, axis, [(i, (i + by) % size) for i in range(size)])  8.83 us
    dot_general x1, matrix products, shards(): lax.dot_general(d_qkv, weights, contract_last, preferred_element_type=jnp...  8.52 us
  transfers between devices with their start and end apart: 7, of which 7 were waited for; matrix products, arithmetic and copies ran while one was open for 12% of the time, Pallas kernels for 0%

commit v1 on v0

v1 whole, which is shorter than its diff:
```python
import functools
import math

import jax
import jax.numpy as jnp
from jax import lax
from jax.experimental import pallas as pl
from jax.experimental.pallas import tpu as pltpu
from jax.sharding import PartitionSpec as P

D = 12288
HEAD_DIM = 128
EPS = 1e-05
ROWS = 128
WIDTH = 384
HALF = 64
QUARTER = 32
THREE = 3 * HEAD_DIM
SCALE = 1.0 / math.sqrt(HEAD_DIM)
MESH = pl.DeviceIdType.MESH
F32 = jnp.float32
BF16 = jnp.bfloat16
NT = (((1,), (1,)), ((), ()))
TN = (((0,), (0,)), ((), ()))
N_MESSAGES = 160

OFFSET = (0, 1, 3, 2)


def mm(a, b, dims=None):
    if dims is None:
        return jnp.dot(a, b, preferred_element_type=F32)
    return lax.dot_general(a, b, dims, preferred_element_type=F32)


class Wire:
    def __init__(self, send_sems, recv_sems):
        self.send_sems, self.recv_sems = send_sems, recv_sems
        self.count = 0
        self.open = []

    def send(self, src, dst, device):
        copy = pltpu.make_async_remote_copy(
            src_ref=src,
            dst_ref=dst,
            send_sem=self.send_sems.at[self.count],
            recv_sem=self.recv_sems.at[self.count],
            device_id=device,
            device_id_type=MESH,
        )
        self.count += 1
        copy.start()
        self.open.append(copy)
        return copy

    def drain(self):
        for copy in self.open:
            copy.wait_send()
        self.open = []


def wait_all(copies):
    for copy in copies:
        copy.wait_recv()


class Gather:
    def __init__(self, wire, near, slots):
        self.wire, self.near, self.slots = wire, near, slots

    def first(self, own):
        s, w, n = self.slots, self.wire, self.near
        a, b = pl.ds(0, HALF), pl.ds(HALF, HALF)
        self.one = [
            w.send(own.at[a], s.at[0, 2, a], n["xp"]),
            w.send(own.at[a], s.at[0, 1, a], n["xm"]),
            w.send(own.at[b], s.at[2, 0, b], n["yp"]),
            w.send(own.at[b], s.at[1, 0, b], n["ym"]),
        ]

    def second(self):
        s, w, n = self.slots, self.wire, self.near
        wait_all(self.one)
        a0, a1 = pl.ds(0, QUARTER), pl.ds(QUARTER, QUARTER)
        b0, b1 = pl.ds(HALF, QUARTER), pl.ds(HALF + QUARTER, QUARTER)
        self.two = [
            w.send(s.at[0, 2, a0], s.at[0, 3, a0], n["xp"]),
            w.send(s.at[0, 1, a1], s.at[0, 3, a1], n["xm"]),
            w.send(s.at[2, 0, b0], s.at[3, 0, b0], n["yp"]),
            w.send(s.at[1, 0, b1], s.at[3, 0, b1], n["ym"]),
        ]
        self.three = [self._across(pl.ds(0, 3)), None]

    def third(self):
        wait_all(self.two)
        self.three[1] = self._across(pl.ds(3, 1))

    def _across(self, part):
        s, w, n = self.slots, self.wire, self.near
        a, b = pl.ds(0, HALF), pl.ds(HALF, HALF)
        return [
            w.send(s.at[0, part, a], s.at[2, part, a], n["yp"]),
            w.send(s.at[0, part, a], s.at[1, part, a], n["ym"]),
            w.send(s.at[part, 0, b], s.at[part, 2, b], n["xp"]),
            w.send(s.at[part, 0, b], s.at[part, 1, b], n["xm"]),
        ]

    def fourth(self, which):
        s, w, n = self.slots, self.wire, self.near
        wait_all(self.three[which])
        part = (pl.ds(0, 3), pl.ds(3, 1))[which]
        a0, a1 = pl.ds(0, QUARTER), pl.ds(QUARTER, QUARTER)
        b0, b1 = pl.ds(HALF, QUARTER), pl.ds(HALF + QUARTER, QUARTER)
        copies = [
            w.send(s.at[2, part, a0], s.at[3, part, a0], n["yp"]),
            w.send(s.at[1, part, a1], s.at[3, part, a1], n["ym"]),
            w.send(s.at[part, 2, b0], s.at[part, 3, b0], n["xp"]),
            w.send(s.at[part, 1, b1], s.at[part, 3, b1], n["xm"]),
        ]
        if which == 0:
            self.four = copies
        else:
            self.four += copies

    def finish(self):
        wait_all(self.four)


def add_into(target, *terms):
    total = target[...].astype(F32)
    for term in terms:
        total = total + term[...].astype(F32)
    target[...] = total.astype(BF16)


class Scatter:
    def __init__(self, wire, near, parts, a1, a2, b1, b2):
        self.wire, self.near, self.parts = wire, near, parts
        self.a1, self.a2, self.b1, self.b2 = a1, a2, b1, b2

    def _long(self, half, pos, rows):
        rows = pl.ds(half * HALF + rows, QUARTER)
        if half == 0:
            return self.parts.at[pos, pl.ds(0, 4), rows]
        return self.parts.at[pl.ds(0, 4), pos, rows]

    def _short(self, half, pos, rows):
        rows = pl.ds(half * HALF + rows, QUARTER)
        if half == 0:
            return self.parts.at[0, pos, rows]
        return self.parts.at[pos, 0, rows]

    def _ways(self, half, long):
        axis = "y" if (half == 0) == long else "x"
        return self.near[axis + "p"], self.near[axis + "m"]

    def _start(self, half, view, r1, r2, long):
        up, down = self._ways(half, long)
        w, lead = self.wire, (pl.ds(0, 4),) if long else ()
        lo, hi = pl.ds(0, QUARTER), pl.ds(QUARTER, QUARTER)
        one = [
            w.send(view(half, 3, 0), r1.at[half, 0], up),
            w.send(view(half, 3, QUARTER), r1.at[half, 1], down),
        ]
        two = [
            w.send(view(half, 1, QUARTER), r2.at[(half, 0) + lead + (hi,)], up),
            w.send(view(half, 2, 0), r2.at[(half, 1) + lead + (lo,)], down),
        ]
        return one, two

    def _pass(self, half, view, r1, r2, long, one, two):
        up, down = self._ways(half, long)
        w, lead = self.wire, (pl.ds(0, 4),) if long else ()
        lo, hi = pl.ds(0, QUARTER), pl.ds(QUARTER, QUARTER)
        one[0].wait_recv()
        add_into(view(half, 1, 0), r1.at[half, 0])
        two.append(w.send(view(half, 1, 0), r2.at[(half, 0) + lead + (lo,)], up))
        one[1].wait_recv()
        add_into(view(half, 2, QUARTER), r1.at[half, 1])
        two.append(w.send(view(half, 2, QUARTER), r2.at[(half, 1) + lead + (hi,)], down))

    def first(self):
        self.long = [self._start(h, self._long, self.a1, self.a2, True) for h in (0, 1)]

    def second(self):
        for h in (0, 1):
            self._pass(h, self._long, self.a1, self.a2, True, *self.long[h])

    def third(self):
        self.short = []
        for h in (0, 1):
            wait_all(self.long[h][1])
            for pos in (3, 1, 2, 0):
                for q in (0, QUARTER):
                    rows = pl.ds(q, QUARTER)
                    add_into(
                        self._short(h, pos, q),
                        self.a2.at[h, 0, pos, rows],
                        self.a2.at[h, 1, pos, rows],
                    )
            self.short.append(self._start(h, self._short, self.b1, self.b2, False))

    def fourth(self):
        for h in (0, 1):
            self._pass(h, self._short, self.b1, self.b2, False, *self.short[h])

    def finish(self):
        halves = []
        for h in (0, 1):
            wait_all(self.short[h][1])
            own = self.parts[0, 0, pl.ds(h * HALF, HALF)].astype(F32)
            halves.append(own + self.b2[h, 0].astype(F32) + self.b2[h, 1].astype(F32))
        return jnp.concatenate(halves, axis=0)


def partial_sums(slots, sums):
    def body(i, carry):
        one, two = carry
        block = slots[i // 4, i % 4].astype(F32)
        for k in range(WIDTH // 128):
            part = block[:, k * 128 : (k + 1) * 128]
            one, two = one + part, two + part * part
        return one, two

    zero = jnp.zeros((ROWS, 128), F32)
    one, two = lax.fori_loop(0, 16, body, (zero, zero))
    sums[0] = one
    sums[1] = two


def statistics(mine, other):
    center = jnp.sum(mine[0] + other[0], -1, keepdims=True) * (1.0 / D)
    square = jnp.sum(mine[1] + other[1], -1, keepdims=True) * (1.0 / D)
    return center, lax.rsqrt(square - center * center + EPS)


def project(slots, gains, weights, total, center, inv_std, with_gain):
    def body(i, _):
        row, col = i // 2, (i % 2) * 2
        blocks = []
        for k in range(2):
            gain = gains[row, col + k]
            hidden = (slots[row, col + k].astype(F32) - center) * inv_std * gain
            block = hidden.astype(BF16)
            if with_gain:
                high = gain.astype(BF16).astype(F32)
                middle = (gain - high).astype(BF16).astype(F32)
                low = gain - high - middle
                at = lax.broadcasted_iota(jnp.int32, (16, WIDTH), 0)
                extra = jnp.where(at == 0, high, jnp.where(at == 1, middle, low))
                extra = jnp.where(at < 3, extra, 0.0)
                block = jnp.concatenate([block, extra.astype(BF16)], axis=0)
            blocks.append(block)
        lhs = jnp.concatenate(blocks, axis=1)
        rhs = weights[row, pl.ds(col, 2)].reshape(2 * WIDTH, 2 * THREE)
        value = mm(lhs, rhs)

        @pl.when(i == 0)
        def _():
            total[...] = value

        @pl.when(i > 0)
        def _():
            total[...] += value

        return 0

    lax.fori_loop(0, 8, body, 0)


def visible_pairs(documents):
    across = jnp.broadcast_to(documents, (ROWS, ROWS))
    down = across.T
    query = lax.broadcasted_iota(jnp.int32, (ROWS, ROWS), 0)
    key = lax.broadcasted_iota(jnp.int32, (ROWS, ROWS), 1)
    return (key <= query) & (across == down)


def probabilities(queries, keys, visible):
    scores = jnp.where(visible, mm(queries, keys, NT) * SCALE, -1e30)
    exponent = jnp.exp(scores - jnp.max(scores, -1, keepdims=True))
    return exponent / jnp.sum(exponent, -1, keepdims=True)


def kernel(
    x_prev, x_saved, g_next, w_qkv, w_out, gain, doc_ids,
    y_out, grad_out,
    sb, sg, sf, weights, w_o, gains, part_d, part_y,
    da1, da2, db1, db2, ya1, ya2, yb1, yb2,
    sums, sums_in, total_b, total_f, qkv_in, d_o, d_o_in, d_cat, o_cat,
    corr, corr_in,
    send_sems, recv_sems, local_sems, swap_send, swap_recv,
):
    z, t = lax.axis_index("pipe"), lax.axis_index("tp")
    core, x, y = t % 2, (t // 2) % 4, t // 8
    planes = lax.axis_size("pipe")

    def at(dy, dx):
        return (z, (((y + dy) % 4) * 4 + (x + dx) % 4) * 2 + core)

    partner = (z, t + 1 - 2 * core)
    above, below = ((z + 1) % planes, t), ((z + planes - 1) % planes, t)
    near = {"xp": at(0, 1), "xm": at(0, 3), "yp": at(1, 0), "ym": at(3, 0)}
    x_far, y_far = at(0, 2), at(2, 0)

    barrier = pltpu.get_barrier_semaphore()
    everyone = [partner, above, below, x_far, y_far, *near.values()]
    for device in everyone:
        pl.semaphore_signal(barrier, inc=1, device_id=device, device_id_type=MESH)
    pl.semaphore_wait(barrier, len(everyone))

    wire = Wire(send_sems, recv_sems)
    gb, gg, gf = (Gather(wire, near, slots) for slots in (sb, sg, sf))
    rd = Scatter(wire, near, part_d, da1, da2, db1, db2)
    ry = Scatter(wire, near, part_y, ya1, ya2, yb1, yb2)

    own_b = pltpu.make_async_copy(x_saved, sb.at[0, 0], local_sems.at[0])
    own_b.start()
    gb.first(x_saved)
    shift_g = wire.send(g_next, sg.at[0, 0], below)
    shift_f = wire.send(x_prev, sf.at[0, 0], above)
    own_cols, their_cols = pl.ds(0, THREE), pl.ds(THREE, THREE)
    own_rows, their_rows = pl.ds(0, HEAD_DIM), pl.ds(HEAD_DIM, HEAD_DIM)
    for py in range(4):
        for px in range(4):
            chip = ((y + OFFSET[py]) % 4) * 4 + (x + OFFSET[px]) % 4
            pltpu.make_async_copy(
                w_qkv.at[chip, core], weights.at[py, px, :, own_cols], local_sems.at[1]
            ).start()
            pltpu.make_async_remote_copy(
                src_ref=w_qkv.at[chip, 1 - core],
                dst_ref=weights.at[py, px, :, their_cols],
                send_sem=swap_send.at[0],
                recv_sem=swap_recv.at[0],
                device_id=partner,
                device_id_type=MESH,
            ).start()
            pltpu.make_async_copy(
                gain.at[chip * 2 + core], gains.at[py, px], local_sems.at[3]
            ).start()
    own_b.wait()

    gb.second()
    for py in range(4):
        for px in range(4):
            chip = ((y + OFFSET[py]) % 4) * 4 + (x + OFFSET[px]) % 4
            mine = pl.multiple_of((chip * 2 + core) * WIDTH, 128)
            theirs = pl.multiple_of((chip * 2 + 1 - core) * WIDTH, 128)
            pltpu.make_async_copy(
                w_out.at[:, pl.ds(mine, WIDTH)], w_o.at[py, px, own_rows], local_sems.at[2]
            ).start()
            pltpu.make_async_remote_copy(
                src_ref=w_out.at[:, pl.ds(theirs, WIDTH)],
                dst_ref=w_o.at[py, px, their_rows],
                send_sem=swap_send.at[1],
                recv_sem=swap_recv.at[1],
                device_id=partner,
                device_id_type=MESH,
            ).start()
    gb.third()
    shift_g.wait_recv()
    gg.first(sg.at[0, 0])
    gb.fourth(0)
    gg.second()
    gb.fourth(1)
    gg.third()
    shift_f.wait_recv()

    def swapped(ref, which):
        return pltpu.make_async_remote_copy(
            src_ref=ref,
            dst_ref=ref,
            send_sem=swap_send.at[which],
            recv_sem=swap_recv.at[which],
            device_id=partner,
            device_id_type=MESH,
        )

    gb.finish()
    partial_sums(sb, sums.at[0])
    stats = wire.send(sums.at[0], sums_in.at[0], partner)
    gf.first(sf.at[0, 0])
    pltpu.make_async_copy(gains, gains, local_sems.at[3]).wait()
    half_w = weights.at[:, :, :, own_cols]
    pltpu.make_async_copy(half_w, half_w, local_sems.at[1]).wait()
    swap_w = swapped(weights.at[:, :, :, their_cols], 0)
    swap_w.wait_recv()
    stats.wait_recv()
    center_b, inv_std_b = statistics(sums[0], sums_in[0])
    project(sb, gains, weights, total_b, center_b, inv_std_b, True)
    trade = wire.send(total_b.at[pl.ds(0, ROWS), their_cols], qkv_in.at[0], partner)
    gg.fourth(0)
    gg.fourth(1)
    gf.second()
    trade.wait_recv()
    qkv_b = total_b[pl.ds(0, ROWS), own_cols] + qkv_in[0]
    low_b = qkv_b.astype(BF16)
    queries, keys, values = (low_b[:, k * HEAD_DIM : (k + 1) * HEAD_DIM] for k in range(3))
    probs = probabilities(queries, keys, visible_pairs(doc_ids[pl.ds(1, 1)]))
    probs_low = probs.astype(BF16)
    gf.third()

    gg.finish()
    half_o = w_o.at[:, :, own_rows]
    pltpu.make_async_copy(half_o, half_o, local_sems.at[2]).wait()
    swap_o = swapped(w_o.at[:, :, their_rows], 1)
    swap_o.wait_recv()

    def output_gradient(i, total):
        row, col = i // 2, (i % 2) * 2
        lhs = jnp.concatenate([sg[row, col], sg[row, col + 1]], axis=1)
        rhs = jnp.concatenate([w_o[row, col], w_o[row, col + 1]], axis=1)
        return total + mm(lhs, rhs, NT)

    d_o[...] = lax.fori_loop(0, 8, output_gradient, jnp.zeros((ROWS, 2 * HEAD_DIM), F32))
    trade = wire.send(d_o.at[:, their_rows], d_o_in, partner)
    gf.fourth(0)
    gf.fourth(1)
    trade.wait_recv()
    d_low = (d_o[:, own_rows] + d_o_in[...]).astype(BF16)
    d_values = mm(probs_low, d_low, TN).astype(BF16)
    d_probs = mm(d_low, values, NT)
    d_scores = probs * (d_probs - jnp.sum(d_probs * probs, -1, keepdims=True)) * SCALE
    d_scores = d_scores.astype(BF16)
    d_queries = mm(d_scores, keys).astype(BF16)
    d_keys = mm(d_scores, queries, TN).astype(BF16)
    d_own = jnp.concatenate([d_queries, d_keys, d_values], axis=1)
    d_cat[:, own_cols] = d_own
    trade = wire.send(d_cat.at[:, own_cols], d_cat.at[:, their_cols], partner)
    along_qkv = jnp.sum(d_own.astype(F32) * qkv_b, -1, keepdims=True)
    trade.wait_recv()

    d_all = d_cat[...]
    for py, px in ((3, 0), (3, 2), (0, 2), (1, 2), (2, 2), (1, 0), (2, 0), (0, 0)):
        rhs = weights[py, pl.ds(px, 2)].reshape(2 * WIDTH, 2 * THREE)
        value = mm(d_all, rhs, NT).astype(BF16)
        part_d[py, px] = value[:, :WIDTH]
        part_d[py, px + 1] = value[:, WIDTH:]
    rd.first()

    gain_w = jnp.sum(total_b[pl.ds(ROWS, 8)], 0, keepdims=True)
    along_gain = jnp.sum(d_all.astype(F32) * gain_w, -1, keepdims=True)
    lane = lax.broadcasted_iota(jnp.int32, (ROWS, 128), 1)
    both = jnp.where(lane == 0, along_gain, jnp.where(lane == 1, along_qkv, 0.0))
    corr[0] = both.T[:8]
    corr_copy = wire.send(corr.at[0], corr_in.at[0], partner)

    gf.finish()
    partial_sums(sf, sums.at[1])
    stats = wire.send(sums.at[1], sums_in.at[1], partner)
    corr_copy.wait_recv()
    corr[1] = corr[0] + corr_in[0]
    corr_copies = [
        wire.send(corr.at[1], corr_in.at[k + 1], device)
        for k, device in enumerate((near["xp"], near["xm"], x_far))
    ]
    stats.wait_recv()
    center_f, inv_std_f = statistics(sums[1], sums_in[1])
    project(sf, gains, weights, total_f, center_f, inv_std_f, False)
    trade = wire.send(total_f.at[:, their_cols], qkv_in.at[1], partner)
    rd.second()
    wait_all(corr_copies)
    corr[2] = corr[1] + corr_in[1] + corr_in[2] + corr_in[3]
    corr_copies = [
        wire.send(corr.at[2], corr_in.at[k + 4], device)
        for k, device in enumerate((near["yp"], near["ym"], y_far))
    ]
    trade.wait_recv()
    low_f = (total_f[:, own_cols] + qkv_in[1]).astype(BF16)
    queries, keys, values = (low_f[:, k * HEAD_DIM : (k + 1) * HEAD_DIM] for k in range(3))
    probs = probabilities(queries, keys, visible_pairs(doc_ids[pl.ds(0, 1)]))
    o_cat[:, own_rows] = mm(probs.astype(BF16), values).astype(BF16)
    trade = wire.send(o_cat.at[:, own_rows], o_cat.at[:, their_rows], partner)
    trade.wait_recv()
    o_all = o_cat[...]
    for py, px in ((3, 0), (3, 2), (0, 2), (1, 2), (2, 2), (1, 0), (2, 0), (0, 0)):
        rhs = jnp.concatenate([w_o[py, px], w_o[py, px + 1]], axis=1)
        value = mm(o_all, rhs).astype(BF16)
        part_y[py, px] = value[:, :WIDTH]
        part_y[py, px + 1] = value[:, WIDTH:]
    ry.first()

    rd.third()
    ry.second()
    rd.fourth()
    ry.third()
    wait_all(corr_copies)
    corr[3] = corr[2] + corr_in[4] + corr_in[5] + corr_in[6]
    square = jnp.concatenate([corr[3], jnp.zeros((ROWS - 8, 128), F32)], axis=0).T
    mean_d, mean_dx = square[:, 0:1] * (1.0 / D), square[:, 1:2] * (1.0 / D)
    hidden_gradient = rd.finish()
    x_hat = (sb[0, 0].astype(F32) - center_b) * inv_std_b
    terms = hidden_gradient * gains[0, 0] - mean_d - x_hat * mean_dx
    grad_out[...] = (sg[0, 0].astype(F32) + inv_std_b * terms).astype(BF16)
    ry.fourth()
    swap_w.wait_send()
    swap_o.wait_send()
    y_out[...] = (sf[0, 0].astype(F32) + ry.finish()).astype(BF16)
    wire.drain()


def shards(x_prev, x_saved, g_next, w_qkv, w_out, gain, doc_ids):
    block = (ROWS, WIDTH)
    grid = (4, 4)
    any_spec = pl.BlockSpec(memory_space=pl.ANY)
    vmem_spec = pl.BlockSpec(memory_space=pltpu.VMEM)
    scatter_space = [
        pltpu.VMEM((2, 2, 4, QUARTER, WIDTH), BF16),
        pltpu.VMEM((2, 2, 4, HALF, WIDTH), BF16),
        pltpu.VMEM((2, 2, QUARTER, WIDTH), BF16),
        pltpu.VMEM((2, 2, HALF, WIDTH), BF16),
    ]
    y_out, grad = pl.pallas_call(
        kernel,
        out_shape=[jax.ShapeDtypeStruct(block, BF16)] * 2,
        in_specs=[any_spec] * 6 + [vmem_spec],
        out_specs=[vmem_spec] * 2,
        scratch_shapes=[
            *[pltpu.VMEM(grid + block, BF16)] * 3,
            pltpu.VMEM(grid + (WIDTH, 2 * THREE), BF16),
            pltpu.VMEM(grid + (2 * HEAD_DIM, WIDTH), BF16),
            pltpu.VMEM(grid + (1, WIDTH), F32),
            *[pltpu.VMEM(grid + block, BF16)] * 2,
            *scatter_space,
            *scatter_space,
            pltpu.VMEM((2, 2, ROWS, 128), F32),
            pltpu.VMEM((2, 2, ROWS, 128), F32),
            pltpu.VMEM((ROWS + 16, 2 * THREE), F32),
            pltpu.VMEM((ROWS, 2 * THREE), F32),
            pltpu.VMEM((2, ROWS, THREE), F32),
            pltpu.VMEM((ROWS, 2 * HEAD_DIM), F32),
            pltpu.VMEM((ROWS, HEAD_DIM), F32),
            pltpu.VMEM((ROWS, 2 * THREE), BF16),
            pltpu.VMEM((ROWS, 2 * HEAD_DIM), BF16),
            pltpu.VMEM((4, 8, 128), F32),
            pltpu.VMEM((7, 8, 128), F32),
            pltpu.SemaphoreType.DMA((N_MESSAGES,)),
            pltpu.SemaphoreType.DMA((N_MESSAGES,)),
            pltpu.SemaphoreType.DMA((4,)),
            pltpu.SemaphoreType.DMA((2,)),
            pltpu.SemaphoreType.DMA((2,)),
        ],
        compiler_params=pltpu.CompilerParams(
            collective_id=0, has_side_effects=True, vmem_limit_bytes=56 * 2**20
        ),
        name="section",
    )(
        x_prev[0],
        x_saved[0],
        g_next[0],
        w_qkv.reshape(16, 2, WIDTH, THREE),
        w_out[0],
        gain.reshape(32, 1, WIDTH),
        doc_ids[0],
    )
    return y_out[None], grad[None]


def solution(mesh):
    in_specs = (
        P("pipe", None, "tp"),
        P("pipe", None, "tp"),
        P("pipe", None, "tp"),
        P("pipe", None, "tp", None),
        P("pipe", "tp", None),
        P("pipe", None),
        P("pipe", None, None),
    )
    out_specs = (P("pipe", None, "tp"), P("pipe", None, "tp"))
    return jax.shard_map(shards, mesh=mesh, in_specs=in_specs, out_specs=out_specs, check_vma=False)
```

time: 397 us -> 78.1 us (0.20)
  waiting for transfers between devices: 325 us -> 0 us
  Pallas kernels: 0 us -> 74 us
  matrix products: 26.5 us -> 0 us
  other arithmetic: 16.4 us -> 0 us
  between operations: 14 us -> 0.64 us
  starting transfers between devices: 6.4 us -> 0 us
  local copies, waits for them, and re-layouts: 7.97 us -> 3.09 us
    all_gather x3 -> x0, waiting for transfers between devices: 126 us -> none  [the longest x1 43.4 us: shards(): lax.all_gather(incoming_gradient, 'tp', axis=1, tiled=True)]
    psum x1 -> x0, waiting for transfers between devices: 104 us -> none  [shards(): lax.psum(d_partial.astype(jnp.bfloat16), 'tp').astype(jnp.float32)]
    unnamed x6 -> x0, waiting for transfers between devices: 87.2 us -> none
    pallas_call x0 -> x1, Pallas kernels: none -> 74 us  [shards(): pl.pallas_call(kernel, out_shape=[jax.ShapeDtypeStruct(block, BF16)] * 2,...]
    dot_general x11 -> x0, matrix products: 26.5 us -> none  [the longest x1 8.52 us: shards(): lax.dot_general(d_qkv, weights, contract_last, preferred_element_type=jnp...]
    reduce_sum x7 -> x0, other arithmetic: 14.9 us -> none  [the longest x2 5.17 us: layer_stats(): square = jnp.mean(values * values, -1, keepdims=True)]
    ppermute x2 -> x0, waiting for transfers between devices: 8.83 us -> none  [shifted(): lax.ppermute(value, axis, [(i, (i + by) % size) for i in range(size)])]
    ppermute x2 -> x0, starting transfers between devices: 6.02 us -> none  [shifted(): lax.ppermute(value, axis, [(i, (i + by) % size) for i in range(size)])]
  transfers between devices with their start and end apart: 7 -> 0, of which waited for: 7 -> 0; matrix products, arithmetic and copies ran while one was open for 12% -> 0% of each run, Pallas kernels for 0% -> 0%
where the time goes in v1:
time: 78.1 us; the launch traced here: 77.7 us
  Pallas kernels  74 us (95%)
  local copies, waits for them, and re-layouts  3.09 us (4%)
    pallas_call x1, Pallas kernels, shards(): pl.pallas_call(kernel, out_shape=[jax.ShapeDtypeStruct(block, BF16)] * 2,...  74 us
    unnamed x2, local copies, waits for them, and re-layouts  3.09 us

profile of v1, /device:TPU:2, one launch (start us, length us, event | category | flops | bytes accessed | tf_op | source)
XLA Modules:
  0.0 77.7 jit_solution(1196991802625564458)
XLA Ops:
  0.6 74.0 %section.1 = (bf16[128,384]{1,0:T(8,128)(2,1)}, bf16[128,384]{1,0:T(8,128)(2,1)}) custom-call(bf16[128,384]{1,0:T(8,128)(2,1)} %bitcast.11, bf16[128,384]{1,0:T(8,128)(2,1)} %bitcast.12, bf16[128,384]{1,0:T(8,128)(2,1)} %bitcast.13, bf16[16,2,384,384]{3,2,1,0:T(8,128)(2,1)} %bitcast.9, bf16[128,12288]{1,0:T(8,128)(2,1)} %bitcast.10, f32[32,1,384]{2,1,0:T(1,128)} %bitcast.16, ...), custom_call_target="tpu_custom_call" | custom-call | tf_op jit(solution)/shard_map/section/pallas_call | solution.py:513
  74.6 1.5 %copy.11 = bf16[1,128,384]{2,1,0:T(8,128)(2,1)} copy(bf16[1,128,384]{2,1,0:T(8,128)(2,1)} %bitcast.15) | data formatting | bytes 196608
  76.2 1.5 %copy.12 = bf16[1,128,384]{2,1,0:T(8,128)(2,1)} copy(bf16[1,128,384]{2,1,0:T(8,128)(2,1)} %bitcast.14) | data formatting | bytes 196608

commit v2 on v1

v2 whole, which is shorter than its diff:
```python
import functools
import math

import jax
import jax.numpy as jnp
from jax import lax
from jax.experimental import pallas as pl
from jax.experimental.pallas import tpu as pltpu
from jax.sharding import PartitionSpec as P

D = 12288
HEAD_DIM = 128
EPS = 1e-05
ROWS = 128
WIDTH = 384
HALF = 64
QUARTER = 32
THREE = 3 * HEAD_DIM
SCALE = 1.0 / math.sqrt(HEAD_DIM)
MESH = pl.DeviceIdType.MESH
F32 = jnp.float32
BF16 = jnp.bfloat16
NT = (((1,), (1,)), ((), ()))
TN = (((0,), (0,)), ((), ()))
N_SENDERS, N_RECEIVERS = 20, 46

OFFSET = (0, 1, 3, 2)


def mm(a, b, dims=None):
    if dims is None:
        return jnp.dot(a, b, preferred_element_type=F32)
    return lax.dot_general(a, b, dims, preferred_element_type=F32)


class Wire:
    def __init__(self, send_sems, recv_sems, partner):
        self.send_sems, self.recv_sems, self.partner = send_sems, recv_sems, partner
        self.sends = self.receives = 0

    def sender(self):
        self.sends += 1
        return self.send_sems.at[self.sends - 1]

    def group(self, send_sem=None):
        self.receives += 1
        receiver = self.recv_sems.at[self.receives - 1]
        return Group(self.sender() if send_sem is None else send_sem, receiver, self.partner)

    def send(self, src, dst, device):
        group = self.group()
        group.send(src, dst, device)
        return group


class Group:
    def __init__(self, send_sem, recv_sem, partner):
        self.send_sem, self.recv_sem, self.partner = send_sem, recv_sem, partner

    def _copy(self, src, dst, device):
        return pltpu.make_async_remote_copy(
            src_ref=src,
            dst_ref=dst,
            send_sem=self.send_sem,
            recv_sem=self.recv_sem,
            device_id=device,
            device_id_type=MESH,
        )

    def send(self, src, dst, device):
        self.last = self._copy(src, dst, device)
        self.last.start()

    def received(self, like=None):
        (self.last if like is None else self._copy(like, like, self.partner)).wait_recv()

    def sent(self, like=None):
        (self.last if like is None else self._copy(like, like, self.partner)).wait_send()


class Gather:
    def __init__(self, wire, near, slots):
        self.near, self.slots = near, slots
        self.sender = wire.sender()
        self.one, self.two, self.three, self.more, self.four = (
            wire.group(self.sender) for _ in range(5)
        )

    def first(self, own):
        s, n, g = self.slots, self.near, self.one
        a, b = pl.ds(0, HALF), pl.ds(HALF, HALF)
        g.send(own.at[a], s.at[0, 2, a], n["xp"])
        g.send(own.at[b], s.at[2, 0, b], n["yp"])
        g.send(own.at[a], s.at[0, 1, a], n["xm"])
        g.send(own.at[b], s.at[1, 0, b], n["ym"])

    def second(self):
        s, n, g = self.slots, self.near, self.two
        self.one.received(s.at[0, pl.ds(0, 2)])
        a0, a1 = pl.ds(0, QUARTER), pl.ds(QUARTER, QUARTER)
        b0, b1 = pl.ds(HALF, QUARTER), pl.ds(HALF + QUARTER, QUARTER)
        g.send(s.at[0, 2, a0], s.at[0, 3, a0], n["xp"])
        g.send(s.at[2, 0, b0], s.at[3, 0, b0], n["yp"])
        g.send(s.at[0, 1, a1], s.at[0, 3, a1], n["xm"])
        g.send(s.at[1, 0, b1], s.at[3, 0, b1], n["ym"])
        self._across(self.three, pl.ds(0, 3))

    def third(self):
        self.two.received(self.slots.at[0, 0])
        self._across(self.more, pl.ds(3, 1))

    def _across(self, g, part):
        s, n = self.slots, self.near
        a, b = pl.ds(0, HALF), pl.ds(HALF, HALF)
        g.send(s.at[0, part, a], s.at[2, part, a], n["yp"])
        g.send(s.at[part, 0, b], s.at[part, 2, b], n["xp"])
        g.send(s.at[0, part, a], s.at[1, part, a], n["ym"])
        g.send(s.at[part, 0, b], s.at[part, 1, b], n["xm"])

    def _onward(self, part):
        s, n, g = self.slots, self.near, self.four
        a0, a1 = pl.ds(0, QUARTER), pl.ds(QUARTER, QUARTER)
        b0, b1 = pl.ds(HALF, QUARTER), pl.ds(HALF + QUARTER, QUARTER)
        g.send(s.at[2, part, a0], s.at[3, part, a0], n["yp"])
        g.send(s.at[part, 2, b0], s.at[part, 3, b0], n["xp"])
        g.send(s.at[1, part, a1], s.at[3, part, a1], n["ym"])
        g.send(s.at[part, 1, b1], s.at[part, 3, b1], n["xm"])

    def fourth(self):
        self.three.received(self.slots.at[pl.ds(0, 3), pl.ds(0, 2)])
        self._onward(pl.ds(0, 3))

    def fifth(self):
        self.more.received(self.slots.at[0, pl.ds(0, 2)])
        self._onward(pl.ds(3, 1))

    def finish(self):
        self.four.received(self.slots.at[0])


def add_into(target, *terms):
    total = target[...].astype(F32)
    for term in terms:
        total = total + term[...].astype(F32)
    target[...] = total.astype(BF16)


PIECES = ((3, 1), (1, 2), (0, 1))


class Scatter:
    def __init__(self, wire, near, parts, a1, a2, b1, b2):
        self.near, self.parts = near, parts
        self.a1, self.a2, self.b1, self.b2 = a1, a2, b1, b2
        self.sender = wire.sender()
        self.one = [wire.group(self.sender) for _ in range(4)]
        self.two = [wire.group(self.sender) for _ in range(4)]

    def _part(self, half, pos, rows, k):
        rows = pl.ds(half * HALF + rows, QUARTER)
        if k < 3:
            first, second = pos, pl.ds(*PIECES[k])
        else:
            first, second = 0, pos
        return self.parts.at[(first, second, rows) if half == 0 else (second, first, rows)]

    def _box(self, half, way, rows, k):
        rows = pl.ds(rows, QUARTER)
        if k < 3:
            piece = pl.ds(*PIECES[k])
            return self.a1.at[half, way, piece], self.a2.at[half, way, piece, rows]
        return self.b1.at[half, way], self.b2.at[half, way, rows]

    def _ways(self, half, k):
        axis = "y" if (half == 0) == (k < 3) else "x"
        return self.near[axis + "p"], self.near[axis + "m"]

    def far(self, k, half):
        for way, device in enumerate(self._ways(half, k)):
            self.one[k].send(
                self._part(half, 3, way * QUARTER, k), self._box(half, way, 0, k)[0], device
            )

    def close(self, k, half):
        for way, device in enumerate(self._ways(half, k)):
            rows = (1 - way) * QUARTER
            self.two[k].send(
                self._part(half, 1 + way, rows, k), self._box(half, way, rows, k)[1], device
            )

    def _pass(self, k):
        for half in (0, 1):
            for way, device in enumerate(self._ways(half, k)):
                part = self._part(half, 1 + way, way * QUARTER, k)
                add_into(part, self._box(half, way, 0, k)[0])
                self.two[k].send(part, self._box(half, way, way * QUARTER, k)[1], device)

    def _fold(self, half, pos):
        for q in (0, QUARTER):
            rows = pl.ds(q, QUARTER)
            add_into(
                self._part(half, pos, q, 3),
                self.a2.at[half, 0, pos, rows],
                self.a2.at[half, 1, pos, rows],
            )

    def second(self, k):
        self.one[k].received(self.parts.at[0, pl.ds(0, PIECES[k][1])])
        self._pass(k)

    def third(self):
        self.two[0].received(self.parts.at[0, pl.ds(0, 2)])
        for half in (0, 1):
            self._fold(half, 3)
            self.far(3, half)

    def fourth(self):
        self.two[1].received(self.parts.at[0])
        for half in (0, 1):
            self._fold(half, 1)
            self._fold(half, 2)
            self.close(3, half)

    def fifth(self):
        self.one[3].received(self.parts.at[0, 0])
        self._pass(3)

    def finish(self):
        self.two[2].received(self.parts.at[0, pl.ds(0, 2)])
        self.two[3].received(self.parts.at[0, pl.ds(0, 2)])
        halves = []
        for half in (0, 1):
            total = self.parts[0, 0, pl.ds(half * HALF, HALF)].astype(F32)
            for term in (
                self.a2[half, 0, 0], self.a2[half, 1, 0], self.b2[half, 0], self.b2[half, 1]
            ):
                total = total + term.astype(F32)
            halves.append(total)
        return jnp.concatenate(halves, axis=0)


class AllSum:
    def __init__(self, wire, partner, along_x, along_y, held, box):
        self.held, self.box, self.partner, self.x, self.y = held, box, partner, along_x, along_y
        self.groups = [wire.group() for _ in range(3)]

    def start(self, columns):
        lane = lax.broadcasted_iota(jnp.int32, (ROWS, 128), 1)
        square = jnp.zeros((ROWS, 128), F32)
        for k, column in enumerate(columns):
            square = jnp.where(lane == k, column, square)
        self.held[0] = square.T[:8]
        self.groups[0].send(self.held.at[0], self.box.at[0], self.partner)

    def along_x(self):
        self.groups[0].received()
        self.held[1] = self.held[0] + self.box[0]
        for k, device in enumerate(self.x):
            self.groups[1].send(self.held.at[1], self.box.at[1 + k], device)

    def along_y(self):
        self.groups[1].received(self.box.at[pl.ds(1, 3)])
        self.held[2] = self.held[1] + self.box[1] + self.box[2] + self.box[3]
        for k, device in enumerate(self.y):
            self.groups[2].send(self.held.at[2], self.box.at[4 + k], device)

    def columns(self, count):
        self.groups[2].received(self.box.at[pl.ds(4, 3)])
        total = self.held[2] + self.box[4] + self.box[5] + self.box[6]
        square = jnp.concatenate([total, jnp.zeros((ROWS - 8, 128), F32)], axis=0).T
        return [square[:, k : k + 1] for k in range(count)]

    def sent(self):
        self.groups[0].sent()
        self.groups[1].sent(self.box.at[pl.ds(1, 3)])
        self.groups[2].sent(self.box.at[pl.ds(4, 3)])


def own_sums(block):
    values = block.astype(F32)
    return [jnp.sum(v, -1, keepdims=True) for v in (values, values * values)]


def statistics(total, square):
    center = total * (1.0 / D)
    return center, lax.rsqrt(square * (1.0 / D) - center * center + EPS)


def project(slots, gains, weights, total, center, inv_std, with_gain, first, last):
    def body(i, _):
        row, col = i // 2, (i % 2) * 2
        blocks = []
        for k in range(2):
            gain = gains[row, col + k]
            hidden = (slots[row, col + k].astype(F32) - center) * inv_std * gain
            block = hidden.astype(BF16)
            if with_gain:
                high = gain.astype(BF16).astype(F32)
                middle = (gain - high).astype(BF16).astype(F32)
                low = gain - high - middle
                at = lax.broadcasted_iota(jnp.int32, (16, WIDTH), 0)
                extra = jnp.where(at == 0, high, jnp.where(at == 1, middle, low))
                extra = jnp.where(at < 3, extra, 0.0)
                block = jnp.concatenate([block, extra.astype(BF16)], axis=0)
            blocks.append(block)
        lhs = jnp.concatenate(blocks, axis=1)
        rhs = weights[row, pl.ds(col, 2)].reshape(2 * WIDTH, 2 * THREE)
        value = mm(lhs, rhs)

        @pl.when(i == 0)
        def _():
            total[...] = value

        @pl.when(i > 0)
        def _():
            total[...] += value

        return 0

    lax.fori_loop(first, last, body, 0)


def visible_pairs(documents):
    across = jnp.broadcast_to(documents, (ROWS, ROWS))
    down = across.T
    query = lax.broadcasted_iota(jnp.int32, (ROWS, ROWS), 0)
    key = lax.broadcasted_iota(jnp.int32, (ROWS, ROWS), 1)
    return (key <= query) & (across == down)


def probabilities(queries, keys, visible):
    scores = jnp.where(visible, mm(queries, keys, NT) * SCALE, -1e30)
    exponent = jnp.exp(scores - jnp.max(scores, -1, keepdims=True))
    return exponent / jnp.sum(exponent, -1, keepdims=True)


def kernel(
    x_prev, x_saved, g_next, w_qkv, w_out, gain, doc_ids,
    y_out, grad_out,
    sb, sg, sf, weights, w_o, gains, part_d, part_y,
    da1, da2, db1, db2, ya1, ya2, yb1, yb2,
    qkv_sum_b, qkv_sum_f, qkv_in, d_o, d_o_in, d_cat, o_cat,
    moments_held, moments_box, means_held, means_box,
    send_sems, recv_sems, local_sems,
):
    z, t = lax.axis_index("pipe"), lax.axis_index("tp")
    core, x, y = t % 2, (t // 2) % 4, t // 8
    planes = lax.axis_size("pipe")

    def at(dy, dx):
        return (z, (((y + dy) % 4) * 4 + (x + dx) % 4) * 2 + core)

    partner = (z, t + 1 - 2 * core)
    above, below = ((z + 1) % planes, t), ((z + planes - 1) % planes, t)
    near = {"xp": at(0, 1), "xm": at(0, 3), "yp": at(1, 0), "ym": at(3, 0)}
    x_far, y_far = at(0, 2), at(2, 0)

    barrier = pltpu.get_barrier_semaphore()
    everyone = [partner, above, below, x_far, y_far, *near.values()]
    for device in everyone:
        pl.semaphore_signal(barrier, inc=1, device_id=device, device_id_type=MESH)
    pl.semaphore_wait(barrier, len(everyone))

    wire = Wire(send_sems, recv_sems, partner)
    gb, gf, gg = (Gather(wire, near, slots) for slots in (sb, sf, sg))
    rd = Scatter(wire, near, part_d, da1, da2, db1, db2)
    ry = Scatter(wire, near, part_y, ya1, ya2, yb1, yb2)
    on_x, on_y = (near["xp"], near["xm"], x_far), (near["yp"], near["ym"], y_far)
    moments = AllSum(wire, partner, on_x, on_y, moments_held, moments_box)
    means = AllSum(wire, partner, on_x, on_y, means_held, means_box)
    swap_w, swap_o = wire.group(), wire.group()
    own_cols, their_cols = pl.ds(0, THREE), pl.ds(THREE, THREE)
    own_rows, their_rows = pl.ds(0, HEAD_DIM), pl.ds(HEAD_DIM, HEAD_DIM)

    gb.first(x_saved)
    shift_f = wire.send(x_prev, sf.at[0, 0], above)
    shift_g = wire.send(g_next, sg.at[0, 0], below)
    own_b = pltpu.make_async_copy(x_saved, sb.at[0, 0], local_sems.at[0])
    own_b.start()
    for py in range(4):
        for px in range(4):
            chip = ((y + OFFSET[py]) % 4) * 4 + (x + OFFSET[px]) % 4
            pltpu.make_async_copy(
                w_qkv.at[chip, core], weights.at[py, px, :, own_cols], local_sems.at[1]
            ).start()
            swap_w.send(w_qkv.at[chip, 1 - core], weights.at[py, px, :, their_cols], partner)
            pltpu.make_async_copy(
                gain.at[chip * 2 + core], gains.at[py, px], local_sems.at[3]
            ).start()
    own_b.wait()
    gb.second()
    for py in range(4):
        for px in range(4):
            chip = ((y + OFFSET[py]) % 4) * 4 + (x + OFFSET[px]) % 4
            mine = pl.multiple_of((chip * 2 + core) * WIDTH, 128)
            theirs = pl.multiple_of((chip * 2 + 1 - core) * WIDTH, 128)
            pltpu.make_async_copy(
                w_out.at[:, pl.ds(mine, WIDTH)], w_o.at[py, px, own_rows], local_sems.at[2]
            ).start()
            swap_o.send(w_out.at[:, pl.ds(theirs, WIDTH)], w_o.at[py, px, their_rows], partner)
    gb.third()
    shift_f.received()
    gf.first(sf.at[0, 0])
    moments.start(own_sums(sb[0, 0]) + own_sums(sf[0, 0]))
    gb.fourth()
    moments.along_x()
    gf.second()
    gb.fifth()
    moments.along_y()
    gf.third()
    shift_g.received()
    gg.first(sg.at[0, 0])
    total_b, square_b, total_f, square_f = moments.columns(4)
    center_b, inv_std_b = statistics(total_b, square_b)
    center_f, inv_std_f = statistics(total_f, square_f)

    gb.finish()
    pltpu.make_async_copy(gains, gains, local_sems.at[3]).wait()
    half_w = weights.at[:, :, :, own_cols]
    pltpu.make_async_copy(half_w, half_w, local_sems.at[1]).wait()
    swap_w.received(weights.at[:, :, :, their_cols])
    project(sb, gains, weights, qkv_sum_b, center_b, inv_std_b, True, 0, 3)
    gf.fourth()
    project(sb, gains, weights, qkv_sum_b, center_b, inv_std_b, True, 3, 6)
    gg.second()
    project(sb, gains, weights, qkv_sum_b, center_b, inv_std_b, True, 6, 8)
    trade_b = wire.send(qkv_sum_b.at[pl.ds(0, ROWS), their_cols], qkv_in.at[0], partner)
    gf.fifth()
    trade_b.received()
    qkv_b = qkv_sum_b[pl.ds(0, ROWS), own_cols] + qkv_in[0]
    low_b = qkv_b.astype(BF16)
    queries_b, keys_b, values_b = (low_b[:, k * HEAD_DIM : (k + 1) * HEAD_DIM] for k in range(3))
    probs_b = probabilities(queries_b, keys_b, visible_pairs(doc_ids[pl.ds(1, 1)]))
    gg.third()

    gf.finish()
    project(sf, gains, weights, qkv_sum_f, center_f, inv_std_f, False, 0, 8)
    trade_f = wire.send(qkv_sum_f.at[:, their_cols], qkv_in.at[1], partner)
    gg.fourth()
    gg.fifth()
    trade_f.received()
    low_f = (qkv_sum_f[:, own_cols] + qkv_in[1]).astype(BF16)
    queries, keys, values = (low_f[:, k * HEAD_DIM : (k + 1) * HEAD_DIM] for k in range(3))
    probs = probabilities(queries, keys, visible_pairs(doc_ids[pl.ds(0, 1)]))
    o_cat[:, own_rows] = mm(probs.astype(BF16), values).astype(BF16)
    trade_o = wire.send(o_cat.at[:, own_rows], o_cat.at[:, their_rows], partner)
    half_o = w_o.at[:, :, own_rows]
    pltpu.make_async_copy(half_o, half_o, local_sems.at[2]).wait()
    swap_o.received(w_o.at[:, :, their_rows])
    trade_o.received()
    o_all = o_cat[...]

    def output_blocks(py, px):
        rhs = jnp.concatenate([w_o[py, px], w_o[py, px + 1]], axis=1)
        value = mm(o_all, rhs).astype(BF16)
        part_y[py, px] = value[:, :WIDTH]
        part_y[py, px + 1] = value[:, WIDTH:]

    def scatter(reduction, blocks):
        blocks(3, 2)
        reduction.far(0, 0)
        reduction.far(0, 1)
        blocks(1, 2)
        blocks(2, 2)
        reduction.close(0, 0)
        reduction.far(1, 1)
        blocks(3, 0)
        reduction.close(0, 1)
        reduction.far(1, 0)
        blocks(0, 2)
        reduction.far(2, 0)
        reduction.far(2, 1)
        blocks(1, 0)
        blocks(2, 0)
        reduction.close(1, 0)
        reduction.close(1, 1)
        reduction.close(2, 0)
        blocks(0, 0)
        reduction.close(2, 1)

    scatter(ry, output_blocks)

    gg.finish()

    def output_gradient(i, total):
        row, col = i // 2, (i % 2) * 2
        lhs = jnp.concatenate([sg[row, col], sg[row, col + 1]], axis=1)
        rhs = jnp.concatenate([w_o[row, col], w_o[row, col + 1]], axis=1)
        return total + mm(lhs, rhs, NT)

    d_o[...] = lax.fori_loop(0, 8, output_gradient, jnp.zeros((ROWS, 2 * HEAD_DIM), F32))
    trade_d = wire.send(d_o.at[:, their_rows], d_o_in, partner)
    probs_low = probs_b.astype(BF16)
    ry.second(0)
    trade_d.received()
    d_low = (d_o[:, own_rows] + d_o_in[...]).astype(BF16)
    d_values = mm(probs_low, d_low, TN).astype(BF16)
    d_probs = mm(d_low, values_b, NT)
    d_scores = probs_b * (d_probs - jnp.sum(d_probs * probs_b, -1, keepdims=True)) * SCALE
    d_scores = d_scores.astype(BF16)
    d_queries = mm(d_scores, keys_b).astype(BF16)
    d_keys = mm(d_scores, queries_b, TN).astype(BF16)
    d_own = jnp.concatenate([d_queries, d_keys, d_values], axis=1)
    d_cat[:, own_cols] = d_own
    trade_c = wire.send(d_cat.at[:, own_cols], d_cat.at[:, their_cols], partner)
    ry.second(1)
    along_qkv = jnp.sum(d_own.astype(F32) * qkv_b, -1, keepdims=True)
    trade_c.received()

    d_all = d_cat[...]

    def input_blocks(py, px):
        rhs = weights[py, pl.ds(px, 2)].reshape(2 * WIDTH, 2 * THREE)
        value = mm(d_all, rhs, NT).astype(BF16)
        part_d[py, px] = value[:, :WIDTH]
        part_d[py, px + 1] = value[:, WIDTH:]

    scatter(rd, input_blocks)
    ry.second(2)

    gain_w = jnp.sum(qkv_sum_b[pl.ds(ROWS, 8)], 0, keepdims=True)
    along_gain = jnp.sum(d_all.astype(F32) * gain_w, -1, keepdims=True)
    means.start([along_gain, along_qkv])
    ry.third()
    rd.second(0)
    means.along_x()
    ry.fourth()
    rd.second(1)
    ry.fifth()
    means.along_y()
    rd.second(2)
    rd.third()
    y_out[...] = (sf[0, 0].astype(F32) + ry.finish()).astype(BF16)
    rd.fourth()
    mean_d, mean_dx = means.columns(2)
    x_hat = (sb[0, 0].astype(F32) - center_b) * inv_std_b
    rest = sg[0, 0].astype(F32) - inv_std_b * (mean_d + x_hat * mean_dx) * (1.0 / D)
    rd.fifth()
    all_sent = weights.at[:, 0, pl.ds(0, 240)]
    for one in (gb, gf, gg, ry):
        Group(one.sender, None, partner).sent(all_sent)
    for one in (
        shift_f, shift_g, trade_b, trade_f, trade_o, trade_d, trade_c, moments, means
    ):
        one.sent()
    swap_w.sent(weights.at[:, :, :, their_cols])
    swap_o.sent(w_o.at[:, :, their_rows])
    grad_out[...] = (rest + inv_std_b * (rd.finish() * gains[0, 0])).astype(BF16)
    Group(rd.sender, None, partner).sent(all_sent)


def place(y_ref, grad_ref, y_out, grad_out, sems):
    copies = [
        pltpu.make_async_copy(y_ref, y_out, sems.at[0]),
        pltpu.make_async_copy(grad_ref, grad_out, sems.at[1]),
    ]
    for copy in copies:
        copy.start()
    for copy in copies:
        copy.wait()


def shards(x_prev, x_saved, g_next, w_qkv, w_out, gain, doc_ids):
    block = (ROWS, WIDTH)
    grid = (4, 4)
    any_spec = pl.BlockSpec(memory_space=pl.ANY)
    vmem_spec = pl.BlockSpec(memory_space=pltpu.VMEM)
    scatter_space = [
        pltpu.VMEM((2, 2, 4, QUARTER, WIDTH), BF16),
        pltpu.VMEM((2, 2, 4, HALF, WIDTH), BF16),
        pltpu.VMEM((2, 2, QUARTER, WIDTH), BF16),
        pltpu.VMEM((2, 2, HALF, WIDTH), BF16),
    ]
    y_out, grad = pl.pallas_call(
        kernel,
        out_shape=[jax.ShapeDtypeStruct(block, BF16)] * 2,
        in_specs=[any_spec] * 6 + [vmem_spec],
        out_specs=[vmem_spec] * 2,
        scratch_shapes=[
            *[pltpu.VMEM(grid + block, BF16)] * 3,
            pltpu.VMEM(grid + (WIDTH, 2 * THREE), BF16),
            pltpu.VMEM(grid + (2 * HEAD_DIM, WIDTH), BF16),
            pltpu.VMEM(grid + (1, WIDTH), F32),
            *[pltpu.VMEM(grid + block, BF16)] * 2,
            *scatter_space,
            *scatter_space,
            pltpu.VMEM((ROWS + 16, 2 * THREE), F32),
            pltpu.VMEM((ROWS, 2 * THREE), F32),
            pltpu.VMEM((2, ROWS, THREE), F32),
            pltpu.VMEM((ROWS, 2 * HEAD_DIM), F32),
            pltpu.VMEM((ROWS, HEAD_DIM), F32),
            pltpu.VMEM((ROWS, 2 * THREE), BF16),
            pltpu.VMEM((ROWS, 2 * HEAD_DIM), BF16),
            *[pltpu.VMEM((3, 8, 128), F32), pltpu.VMEM((7, 8, 128), F32)] * 2,
            pltpu.SemaphoreType.DMA((N_SENDERS,)),
            pltpu.SemaphoreType.DMA((N_RECEIVERS,)),
            pltpu.SemaphoreType.DMA((4,)),
        ],
        compiler_params=pltpu.CompilerParams(
            collective_id=0, has_side_effects=True, vmem_limit_bytes=56 * 2**20
        ),
        name="section",
    )(
        x_prev[0],
        x_saved[0],
        g_next[0],
        w_qkv.reshape(16, 2, WIDTH, THREE),
        w_out[0],
        gain.reshape(32, 1, WIDTH),
        doc_ids[0],
    )
    y_out, grad = pl.pallas_call(
        place,
        out_shape=[jax.ShapeDtypeStruct(block, BF16)] * 2,
        in_specs=[vmem_spec] * 2,
        out_specs=[any_spec] * 2,
        scratch_shapes=[pltpu.SemaphoreType.DMA((2,))],
        name="place",
    )(y_out, grad)
    return y_out[None], grad[None]


def solution(mesh):
    in_specs = (
        P("pipe", None, "tp"),
        P("pipe", None, "tp"),
        P("pipe", None, "tp"),
        P("pipe", None, "tp", None),
        P("pipe", "tp", None),
        P("pipe", None),
        P("pipe", None, None),
    )
    out_specs = (P("pipe", None, "tp"), P("pipe", None, "tp"))
    return jax.shard_map(shards, mesh=mesh, in_specs=in_specs, out_specs=out_specs, check_vma=False)
```

time: 78.1 us -> 68.9 us (0.88)
  Pallas kernels: 74 us -> 68 us
  local copies, waits for them, and re-layouts: 3.09 us -> 0 us
    pallas_call x1, Pallas kernels: 74 us -> 66.4 us  [shards(): pl.pallas_call(kernel, out_shape=[jax.ShapeDtypeStruct(block, BF16)] * 2,...]
    unnamed x2 -> x0, local copies, waits for them, and re-layouts: 3.09 us -> none
    pallas_call x0 -> x1, Pallas kernels: none -> 1.63 us  [shards(): pl.pallas_call(place, out_shape=[jax.ShapeDtypeStruct(block, BF16)] * 2,...]
where the time goes in v2:
time: 68.9 us; the launch traced here: 68.6 us
  Pallas kernels  68 us (99%)
    pallas_call x1, Pallas kernels, shards(): pl.pallas_call(kernel, out_shape=[jax.ShapeDtypeStruct(block, BF16)] * 2,...  66.4 us
    pallas_call x1, Pallas kernels, shards(): pl.pallas_call(place, out_shape=[jax.ShapeDtypeStruct(block, BF16)] * 2,...  1.63 us

profile of v2, /device:TPU:2, one launch (start us, length us, event | category | flops | bytes accessed | tf_op | source)
XLA Modules:
  0.0 68.6 jit_solution(11092706979503262224)
XLA Ops:
  0.6 66.4 %section.1 = (bf16[128,384]{1,0:T(8,128)(2,1)}, bf16[128,384]{1,0:T(8,128)(2,1)}) custom-call(bf16[128,384]{1,0:T(8,128)(2,1)} %bitcast.11, bf16[128,384]{1,0:T(8,128)(2,1)} %bitcast.12, bf16[128,384]{1,0:T(8,128)(2,1)} %bitcast.13, bf16[16,2,384,384]{3,2,1,0:T(8,128)(2,1)} %bitcast.9, bf16[128,12288]{1,0:T(8,128)(2,1)} %bitcast.10, f32[32,1,384]{2,1,0:T(1,128)} %bitcast.14, ...), custom_call_target="tpu_custom_call" | custom-call | tf_op jit(solution)/shard_map/section/pallas_call | solution.py:574
  67.0 1.6 %place.1 = (bf16[128,384]{1,0:T(8,128)(2,1)}, bf16[128,384]{1,0:T(8,128)(2,1)}) custom-call(bf16[128,384]{1,0:T(8,128)(2,1)} %get-tuple-element.6.y_ref, bf16[128,384]{1,0:T(8,128)(2,1)} %get-tuple-element.7.grad_ref), custom_call_target="tpu_custom_call" | custom-call | tf_op jit(solution)/shard_map/place/pallas_call | solution.py:612

commit v3 on v2

--- a/solution.py
+++ b/solution.py
@@ -288,7 +288,7 @@
 
 def project(slots, gains, weights, total, center, inv_std, with_gain, first, last):
     def body(i, _):
-        row, col = i // 2, (i % 2) * 2
+        row, col = i % 4, (i // 4) * 2
         blocks = []
         for k in range(2):
             gain = gains[row, col + k]
@@ -335,12 +335,12 @@
 
 
 def kernel(
-    x_prev, x_saved, g_next, w_qkv, w_out, gain, doc_ids,
+    x_prev, x_saved, g_next, w_qkv, w_out, gain, documents,
     y_out, grad_out,
     sb, sg, sf, weights, w_o, gains, part_d, part_y,
     da1, da2, db1, db2, ya1, ya2, yb1, yb2,
     qkv_sum_b, qkv_sum_f, qkv_in, d_o, d_o_in, d_cat, o_cat,
-    moments_held, moments_box, means_held, means_box,
+    moments_held, moments_box, means_held, means_box, doc_ids,
     send_sems, recv_sems, local_sems,
 ):
     z, t = lax.axis_index("pipe"), lax.axis_index("tp")
@@ -387,6 +387,8 @@
             pltpu.make_async_copy(
                 gain.at[chip * 2 + core], gains.at[py, px], local_sems.at[3]
             ).start()
+    own_docs = pltpu.make_async_copy(documents, doc_ids, local_sems.at[4])
+    own_docs.start()
     own_b.wait()
     gb.second()
     for py in range(4):
@@ -414,39 +416,57 @@
     center_b, inv_std_b = statistics(total_b, square_b)
     center_f, inv_std_f = statistics(total_f, square_f)
 
-    gb.finish()
     pltpu.make_async_copy(gains, gains, local_sems.at[3]).wait()
     half_w = weights.at[:, :, :, own_cols]
     pltpu.make_async_copy(half_w, half_w, local_sems.at[1]).wait()
     swap_w.received(weights.at[:, :, :, their_cols])
-    project(sb, gains, weights, qkv_sum_b, center_b, inv_std_b, True, 0, 3)
+    own_docs.wait()
+
+    def project_b(first, last):
+        project(sb, gains, weights, qkv_sum_b, center_b, inv_std_b, True, first, last)
+
+    def project_f(first, last):
+        project(sf, gains, weights, qkv_sum_f, center_f, inv_std_f, False, first, last)
+
+    project_b(0, 3)
+    gb.finish()
+    project_b(3, 6)
     gf.fourth()
-    project(sb, gains, weights, qkv_sum_b, center_b, inv_std_b, True, 3, 6)
+    gf.fifth()
     gg.second()
-    project(sb, gains, weights, qkv_sum_b, center_b, inv_std_b, True, 6, 8)
+    project_b(6, 8)
     trade_b = wire.send(qkv_sum_b.at[pl.ds(0, ROWS), their_cols], qkv_in.at[0], partner)
-    gf.fifth()
+    project_f(0, 3)
+    gg.third()
+    gf.finish()
+    project_f(3, 8)
+    trade_f = wire.send(qkv_sum_f.at[:, their_cols], qkv_in.at[1], partner)
+
     trade_b.received()
     qkv_b = qkv_sum_b[pl.ds(0, ROWS), own_cols] + qkv_in[0]
     low_b = qkv_b.astype(BF16)
     queries_b, keys_b, values_b = (low_b[:, k * HEAD_DIM : (k + 1) * HEAD_DIM] for k in range(3))
     probs_b = probabilities(queries_b, keys_b, visible_pairs(doc_ids[pl.ds(1, 1)]))
-    gg.third()
-
-    gf.finish()
-    project(sf, gains, weights, qkv_sum_f, center_f, inv_std_f, False, 0, 8)
-    trade_f = wire.send(qkv_sum_f.at[:, their_cols], qkv_in.at[1], partner)
     gg.fourth()
-    gg.fifth()
+
     trade_f.received()
     low_f = (qkv_sum_f[:, own_cols] + qkv_in[1]).astype(BF16)
     queries, keys, values = (low_f[:, k * HEAD_DIM : (k + 1) * HEAD_DIM] for k in range(3))
     probs = probabilities(queries, keys, visible_pairs(doc_ids[pl.ds(0, 1)]))
     o_cat[:, own_rows] = mm(probs.astype(BF16), values).astype(BF16)
     trade_o = wire.send(o_cat.at[:, own_rows], o_cat.at[:, their_rows], partner)
+    gg.fifth()
     half_o = w_o.at[:, :, own_rows]
     pltpu.make_async_copy(half_o, half_o, local_sems.at[2]).wait()
     swap_o.received(w_o.at[:, :, their_rows])
+
+    def output_gradient(i, total):
+        row, col = i % 4, (i // 4) * 2
+        lhs = jnp.concatenate([sg[row, col], sg[row, col + 1]], axis=1)
+        rhs = jnp.concatenate([w_o[row, col], w_o[row, col + 1]], axis=1)
+        return total + mm(lhs, rhs, NT)
+
+    d_o[...] = lax.fori_loop(0, 3, output_gradient, jnp.zeros((ROWS, 2 * HEAD_DIM), F32))
     trade_o.received()
     o_all = o_cat[...]
 
@@ -482,13 +502,7 @@
 
     gg.finish()
 
-    def output_gradient(i, total):
-        row, col = i // 2, (i % 2) * 2
-        lhs = jnp.concatenate([sg[row, col], sg[row, col + 1]], axis=1)
-        rhs = jnp.concatenate([w_o[row, col], w_o[row, col + 1]], axis=1)
-        return total + mm(lhs, rhs, NT)
-
-    d_o[...] = lax.fori_loop(0, 8, output_gradient, jnp.zeros((ROWS, 2 * HEAD_DIM), F32))
+    d_o[...] = lax.fori_loop(3, 8, output_gradient, d_o[...])
     trade_d = wire.send(d_o.at[:, their_rows], d_o_in, partner)
     probs_low = probs_b.astype(BF16)
     ry.second(0)
@@ -574,7 +588,7 @@
     y_out, grad = pl.pallas_call(
         kernel,
         out_shape=[jax.ShapeDtypeStruct(block, BF16)] * 2,
-        in_specs=[any_spec] * 6 + [vmem_spec],
+        in_specs=[any_spec] * 7,
         out_specs=[vmem_spec] * 2,
         scratch_shapes=[
             *[pltpu.VMEM(grid + block, BF16)] * 3,
@@ -592,9 +606,10 @@
             pltpu.VMEM((ROWS, 2 * THREE), BF16),
             pltpu.VMEM((ROWS, 2 * HEAD_DIM), BF16),
             *[pltpu.VMEM((3, 8, 128), F32), pltpu.VMEM((7, 8, 128), F32)] * 2,
+            pltpu.VMEM((2, ROWS), jnp.int32),
             pltpu.SemaphoreType.DMA((N_SENDERS,)),
             pltpu.SemaphoreType.DMA((N_RECEIVERS,)),
-            pltpu.SemaphoreType.DMA((4,)),
+            pltpu.SemaphoreType.DMA((5,)),
         ],
         compiler_params=pltpu.CompilerParams(
             collective_id=0, has_side_effects=True, vmem_limit_bytes=56 * 2**20

time: 68.9 us -> 66.3 us (0.962)
  Pallas kernels: 68 us -> 65.6 us
    pallas_call x1, Pallas kernels: 66.4 us -> 63.9 us  [shards(): pl.pallas_call(kernel, out_shape=[jax.ShapeDtypeStruct(block, BF16)] * 2,...]
where the time goes in v3:
time: 66.3 us; the launch traced here: 66.2 us
  Pallas kernels  65.6 us (99%)
    pallas_call x1, Pallas kernels, shards(): pl.pallas_call(kernel, out_shape=[jax.ShapeDtypeStruct(block, BF16)] * 2,...  63.9 us
    pallas_call x1, Pallas kernels, shards(): pl.pallas_call(place, out_shape=[jax.ShapeDtypeStruct(block, BF16)] * 2,...  1.63 us

profile of v3, /device:TPU:2, one launch (start us, length us, event | category | flops | bytes accessed | tf_op | source)
XLA Modules:
  0.0 66.2 jit_solution(6716581985306050009)
XLA Ops:
  0.6 63.9 %section.1 = (bf16[128,384]{1,0:T(8,128)(2,1)}, bf16[128,384]{1,0:T(8,128)(2,1)}) custom-call(bf16[128,384]{1,0:T(8,128)(2,1)} %bitcast.11, bf16[128,384]{1,0:T(8,128)(2,1)} %bitcast.12, bf16[128,384]{1,0:T(8,128)(2,1)} %bitcast.13, bf16[16,2,384,384]{3,2,1,0:T(8,128)(2,1)} %bitcast.9, bf16[128,12288]{1,0:T(8,128)(2,1)} %bitcast.10, f32[32,1,384]{2,1,0:T(1,128)} %bitcast.14, ...), custom_call_target="tpu_custom_call" | custom-call | tf_op jit(solution)/shard_map/section/pallas_call | solution.py:588
  64.6 1.6 %place.1 = (bf16[128,384]{1,0:T(8,128)(2,1)}, bf16[128,384]{1,0:T(8,128)(2,1)}) custom-call(bf16[128,384]{1,0:T(8,128)(2,1)} %get-tuple-element.6.y_ref, bf16[128,384]{1,0:T(8,128)(2,1)} %get-tuple-element.7.grad_ref), custom_call_target="tpu_custom_call" | custom-call | tf_op jit(solution)/shard_map/place/pallas_call | solution.py:627

commit v4 on v3

--- a/solution.py
+++ b/solution.py
@@ -341,7 +341,7 @@
     da1, da2, db1, db2, ya1, ya2, yb1, yb2,
     qkv_sum_b, qkv_sum_f, qkv_in, d_o, d_o_in, d_cat, o_cat,
     moments_held, moments_box, means_held, means_box, doc_ids,
-    send_sems, recv_sems, local_sems,
+    send_sems, recv_sems, local_sems, ready,
 ):
     z, t = lax.axis_index("pipe"), lax.axis_index("tp")
     core, x, y = t % 2, (t // 2) % 4, t // 8
@@ -356,10 +356,25 @@
     x_far, y_far = at(0, 2), at(2, 0)
 
     barrier = pltpu.get_barrier_semaphore()
-    everyone = [partner, above, below, x_far, y_far, *near.values()]
-    for device in everyone:
-        pl.semaphore_signal(barrier, inc=1, device_id=device, device_id_type=MESH)
-    pl.semaphore_wait(barrier, len(everyone))
+    hello = functools.partial(pl.semaphore_signal, inc=1, device_id_type=MESH)
+    on_plane = [at(0, 1), at(0, 2), at(0, 3), at(1, 0), at(2, 0), at(3, 0)]
+    for device in on_plane:
+        hello(barrier, device_id=(z, device[1] - core))
+    for plane in (above, below):
+        hello(barrier, device_id=(plane[0], t - core + 1))
+
+    @pl.when(core == 1)
+    def _():
+        hello(barrier, device_id=partner)
+
+    @pl.when(core == 0)
+    def _():
+        pl.semaphore_wait(barrier, 2 * len(on_plane) + 1)
+        hello(ready.at[0], device_id=partner)
+
+    @pl.when(core == 1)
+    def _():
+        pl.semaphore_wait(ready.at[0], 1)
 
     wire = Wire(send_sems, recv_sems, partner)
     gb, gf, gg = (Gather(wire, near, slots) for slots in (sb, sf, sg))
@@ -373,8 +388,6 @@
     own_rows, their_rows = pl.ds(0, HEAD_DIM), pl.ds(HEAD_DIM, HEAD_DIM)
 
     gb.first(x_saved)
-    shift_f = wire.send(x_prev, sf.at[0, 0], above)
-    shift_g = wire.send(g_next, sg.at[0, 0], below)
     own_b = pltpu.make_async_copy(x_saved, sb.at[0, 0], local_sems.at[0])
     own_b.start()
     for py in range(4):
@@ -387,6 +400,17 @@
             pltpu.make_async_copy(
                 gain.at[chip * 2 + core], gains.at[py, px], local_sems.at[3]
             ).start()
+    @pl.when(core == 1)
+    def _():
+        pl.semaphore_wait(barrier, 4)
+        hello(ready.at[1], device_id=partner)
+
+    @pl.when(core == 0)
+    def _():
+        pl.semaphore_wait(ready.at[1], 1)
+
+    shift_f = wire.send(x_prev, sf.at[0, 0], above)
+    shift_g = wire.send(g_next, sg.at[0, 0], below)
     own_docs = pltpu.make_async_copy(documents, doc_ids, local_sems.at[4])
     own_docs.start()
     own_b.wait()
@@ -610,6 +634,7 @@
             pltpu.SemaphoreType.DMA((N_SENDERS,)),
             pltpu.SemaphoreType.DMA((N_RECEIVERS,)),
             pltpu.SemaphoreType.DMA((5,)),
+            pltpu.SemaphoreType.REGULAR((2,)),
         ],
         compiler_params=pltpu.CompilerParams(
             collective_id=0, has_side_effects=True, vmem_limit_bytes=56 * 2**20

time: 66.3 us -> 65.3 us (0.985); the launches traced: 66.2 us -> 64.2 us
  Pallas kernels: 65.6 us -> 63.5 us
    pallas_call x1, Pallas kernels: 63.9 us -> 61.9 us  [shards(): pl.pallas_call(kernel, out_shape=[jax.ShapeDtypeStruct(block, BF16)] * 2,...]
where the time goes in v4:
time: 65.3 us; the launch traced here: 64.2 us
  Pallas kernels  63.5 us (97%)
    pallas_call x1, Pallas kernels, shards(): pl.pallas_call(kernel, out_shape=[jax.ShapeDtypeStruct(block, BF16)] * 2,...  61.9 us
    pallas_call x1, Pallas kernels, shards(): pl.pallas_call(place, out_shape=[jax.ShapeDtypeStruct(block, BF16)] * 2,...  1.63 us

profile of v4, /device:TPU:2, one launch (start us, length us, event | category | flops | bytes accessed | tf_op | source)
XLA Modules:
  0.0 64.2 jit_solution(16597021139665266931)
XLA Ops:
  0.6 61.9 %section.1 = (bf16[128,384]{1,0:T(8,128)(2,1)}, bf16[128,384]{1,0:T(8,128)(2,1)}) custom-call(bf16[128,384]{1,0:T(8,128)(2,1)} %bitcast.11, bf16[128,384]{1,0:T(8,128)(2,1)} %bitcast.12, bf16[128,384]{1,0:T(8,128)(2,1)} %bitcast.13, bf16[16,2,384,384]{3,2,1,0:T(8,128)(2,1)} %bitcast.9, bf16[128,12288]{1,0:T(8,128)(2,1)} %bitcast.10, f32[32,1,384]{2,1,0:T(1,128)} %bitcast.14, ...), custom_call_target="tpu_custom_call" | custom-call | tf_op jit(solution)/shard_map/section/pallas_call | solution.py:612
  62.5 1.6 %place.1 = (bf16[128,384]{1,0:T(8,128)(2,1)}, bf16[128,384]{1,0:T(8,128)(2,1)}) custom-call(bf16[128,384]{1,0:T(8,128)(2,1)} %get-tuple-element.6.y_ref, bf16[128,384]{1,0:T(8,128)(2,1)} %get-tuple-element.7.grad_ref), custom_call_target="tpu_custom_call" | custom-call | tf_op jit(solution)/shard_map/place/pallas_call | solution.py:652
